TPU v7x, 32 devices: a whole 2x2x4 slice. The times are simulated.
32 devices in a mesh: expgrp: 8 (over z, core), patch: 4 (over y, x).
Axes of the slice: x: 2, y: 2, z: 4, core: 2. Of those that a mesh axis runs over, the one named last changes fastest.
Arguments:
- image: float32 [2048, 1024], P(('expgrp', 'patch')), may hold values from -6 to 6
- variance: float32 [2048, 1024], P(('expgrp', 'patch')), may hold values from 0.25 to 4
- block_count: int32 [32, 4], P('expgrp'), may hold values from 0 to 2, as said below
- slot_start: int32 [32, 4], P('expgrp'), may hold values from 0 to 16, as said below
- psf_index: int32 [32], P('expgrp'), may hold values from 0 to 63
- coef_table: float32 [64, 3], replicated, may hold values from 0.1 to 1
Outputs:
- coadd: float32 [1024, 1024], P('patch')
Inputs may be any that keep to these rules, and one draw needn't show every extreme that they name: Each row of block_count sums to 4. In each exposure group one patch owner, drawn per group, receives 2 blocks from every exposure of the group. slot_start + block_count <= 16 for every exposure and owner.
All inputs are finite; a program needn't handle non-finite values.
Results may differ from a plain program's by a relative error of at most 0.0001.
Values sent between devices are 32-bit elements; how exact they have to be, the bound alone decides.
A program may use at most 64 MiB of HBM per device.

v0:
```python
import functools
import math

import jax
import jax.numpy as jnp
import numpy as np
from jax import lax
from jax.experimental import pallas as pl
from jax.experimental.pallas import tpu as pltpu
from jax.sharding import PartitionSpec as P

BLK = 16
CAP = 2
NS = 16
KH = 10
NB = 4
LANES = 128
SIDE = 64


SIGMAS = (0.75, 1.5, 3.0)
BASES = len(SIGMAS)
highest = lax.Precision.HIGHEST
MESH = pl.DeviceIdType.MESH


def np_profile(offsets, deviation):
    every = np.arange(-KH, KH + 1, dtype=np.float64)
    total = np.sum(np.exp(-every * every / (2.0 * deviation * deviation)))
    spacing = offsets.astype(np.float64)
    return np.where(
        np.abs(offsets) <= KH, np.exp(-spacing * spacing / (2.0 * deviation * deviation)) / total, 0.0
    ).astype(np.float32)


def np_row_table():
    row = np.arange(BLK * NB)
    r, n = row // NB, row % NB
    m, k = row // BLK, row % BLK
    same = (n[:, None] == m[None, :]).astype(np.float32)
    return np.concatenate([same * np_profile(k[None, :] - r[:, None], s) for s in SIGMAS], axis=0)


def np_column_table():
    i = np.arange(LANES + 2 * SIDE)[:, None]
    c = np.arange(LANES)[None, :]
    whole = np.concatenate([np_profile(i - SIDE - c, s) for s in SIGMAS], axis=0)
    high = whole.astype(jnp.bfloat16)
    low = (whole - high.astype(np.float32)).astype(jnp.bfloat16)
    return np.concatenate([high, low], axis=1)


def halves(x):
    high = x.astype(jnp.bfloat16)
    return high, (x - high.astype(jnp.float32)).astype(jnp.bfloat16)


def dot(a, b):
    return jnp.dot(a, b, preferred_element_type=jnp.float32)


def kernel(groups, owners, *refs):
    inputs, out, stage = refs[:8], refs[8], refs[9:17]
    (xpad, vbuf, both, dsrc, arrived, rd, cbuf, tbuf, obuf,
     sb, sd, qb, qd, sc, qc, so, qo, sx, qx, local, fetch) = refs[17:]
    loads = [pltpu.make_async_copy(a, b, fetch.at[n]) for n, (a, b) in enumerate(zip(inputs, stage))]
    for n in (1, 2, 3, 4, 5, 0, 6, 7):
        loads[n].start()
    img, var, count, start, psf, coef, rows_t, cols_t = stage
    g, p = lax.axis_index("expgrp"), lax.axis_index("patch")
    devices = groups * owners
    me = g * owners + p
    columns = img.shape[1]
    tiles = columns // LANES
    z, core = g // 2, g % 2

    barrier = pltpu.get_barrier_semaphore()

    @pl.loop(1, devices)
    def _(s):
        k = lax.rem(me + s, devices)
        pl.semaphore_signal(barrier, inc=1, device_id=(k // owners, lax.rem(k, owners)), device_id_type=MESH)

    loads[2].wait()
    loads[3].wait()
    lane = lax.broadcasted_iota(jnp.int32, (1, LANES), 1)
    place = jnp.zeros((1, LANES), jnp.int32)
    block = lax.rem(lane, NB)
    for e in range(owners):
        first = jnp.int32(0)
        for q in range(owners):
            n_here = count[e, q]
            base = q * NS + start[e, q] - first
            inside = (lane // 8 == e) & (block >= first) & (block < first + n_here)
            place = jnp.where(inside, base + block, place)
            first = first + n_here
    dsrc[0] = place
    rd[g] = place
    loads[1].wait()

    for t in range(tiles):
        at = slice(t * LANES, (t + 1) * LANES)
        vbuf[t] = 1.0 / var[:, at]
        for r in range(BLK):
            both[r // 2, 1, (r % 2) * NB:(r % 2) * NB + NB, at] = vbuf[t, pl.ds(r, NB, stride=BLK), :]

    xpad[:, :LANES] = jnp.zeros((NB * BLK, LANES), jnp.float32)
    xpad[:, columns:] = jnp.zeros((NB * BLK, LANES), jnp.float32)
    loads[0].wait()
    xpad[:, SIDE:SIDE + columns] = img[...]
    xh, xl = halves(xpad[...])
    for n in (4, 5, 6):
        loads[n].wait()
    which = psf[p]
    rows = NB * BLK
    ah, al = halves(
        jnp.concatenate([rows_t[b * rows:(b + 1) * rows, :] * coef[b, which] for b in range(BASES)], axis=0)
    )
    yh, yl = halves(dot(ah, xh) + dot(al, xh) + dot(ah, xl))
    wide = LANES + 2 * SIDE
    loads[7].wait()
    double = jnp.zeros((tiles * rows, 2 * LANES), jnp.float32)
    one = jnp.zeros((tiles * rows, LANES), jnp.float32)
    for b in range(BASES):
        def windows(y):
            return jnp.concatenate(
                [y[b * rows:(b + 1) * rows, t * LANES:t * LANES + wide] for t in range(tiles)], axis=0
            )
        double = double + dot(windows(yh), cols_t[b * wide:(b + 1) * wide, :])
        one = one + dot(windows(yl), cols_t[b * wide:(b + 1) * wide, :LANES])
    smooth = double[:, :LANES] + double[:, LANES:] + one
    for t in range(tiles):
        at = slice(t * LANES, (t + 1) * LANES)
        both[:, 0, :, at] = both[:, 1, :, at] * smooth[t * rows:(t + 1) * rows].reshape(rows // 8, 8, LANES)

    pl.semaphore_wait(barrier, devices - 1)

    def send(src, dst, ssem, rsem, k):
        return pltpu.make_async_remote_copy(
            src_ref=src, dst_ref=dst, send_sem=ssem, recv_sem=rsem,
            device_id=(k // owners, lax.rem(k, owners)), device_id_type=MESH,
        )

    def wait_for(ref, sem):
        pltpu.make_async_copy(ref, ref, sem).wait()

    def part(h, k):
        i, j = lax.rem(k, owners), k // owners
        return both.at[owners * h + i, :, :, pl.ds(pl.multiple_of(j * LANES, LANES), LANES)]

    def send_d(s):
        return send(dsrc, rd.at[pl.ds(g, 1)], sd, qd, lax.rem(g + s, groups) * owners + p)

    @pl.loop(1, groups)
    def _(s):
        send_d(s).start()

    own_b = [pltpu.make_async_copy(part(h, me), arrived.at[h, :, me], local.at[h]) for h in range(2)]
    for h in range(2):
        @pl.loop(1, devices)
        def _(s):
            k = lax.rem(me + s, devices)
            send(part(h, k), arrived.at[h, :, me], sb.at[h], qb.at[h], k).start()

        own_b[h].start()

    wait_for(rd.at[pl.ds(0, groups - 1)], qd)

    many = devices * 8
    k_lane = lax.broadcasted_iota(jnp.int32, (1, many), 1)
    goal = jnp.zeros((1, many), jnp.int32)
    run = 8 * owners
    for h in range(groups):
        turned = pltpu.roll(rd[h], (h * run) % LANES, 1)
        goal = jnp.where(k_lane // run == h, jnp.concatenate([turned] * (many // LANES), axis=1), goal)
    slots = owners * NS
    goal = goal + slots * lax.rem(k_lane // NB, 2)
    row = lax.broadcasted_iota(jnp.int32, (2 * slots, many), 0)
    hot = jnp.where(row == goal, 1.0, 0.0).astype(jnp.bfloat16)

    def piece(h, q):
        return cbuf.at[h, :, pl.ds(pl.multiple_of(q * NS, NS), NS), :]

    def landing(h, q):
        return tbuf.at[h, pl.ds(2 * q, 2)]

    def send_c(h, s):
        q = lax.rem(p + s, owners)
        return send(piece(h, q), landing(h, p), sc.at[h, s], qc.at[h, p], g * owners + q)

    own_c = [pltpu.make_async_copy(piece(h, p), landing(h, p), local.at[2 + h]) for h in range(2)]

    def add_up(h):
        wait_for(arrived.at[h, :, pl.ds(0, devices - 1)], qb.at[h])
        own_b[h].wait()
        flux, weight = arrived[h, 0].reshape(many, LANES), arrived[h, 1].reshape(many, LANES)
        high, low = halves(jnp.concatenate([flux, weight], axis=1))
        total = dot(hot, high) + dot(hot, low)
        ratio = total[:, :LANES] / jnp.maximum(total[:, LANES:], 1.0)
        for r2 in range(2):
            cbuf[h, r2] = ratio[r2 * slots:(r2 + 1) * slots]
        for s in range(1, owners):
            send_c(h, s).start()
        own_c[h].start()

    def turn(h):
        for s in range(1, owners):
            e = lax.rem(p + s, owners)
            send(piece(h, p), landing(h, e), sc.at[h, s], qc.at[h, e], g * owners + e).wait_recv()
        own_c[h].wait()
        for r in range(BLK // 2):
            obuf[h, pl.ds(r, NS, stride=BLK // 2), :] = tbuf[h, r]

    def held(h):
        return obuf.at[h].reshape(NS, BLK // 2, LANES)

    def chunk(h, j):
        return out.at[:, h, :, pl.ds(pl.multiple_of(j * LANES, LANES), LANES)]

    chips = groups // 2
    sibling = (z * 2 + 1 - core) * owners + p

    def along(h, s):
        there = lax.rem(z + s, chips) * 2 + core
        return send(held(h), chunk(h, g), so.at[h, s], qo.at[h, s], there * owners + p)

    def across(h, s):
        j = lax.rem(z - s + chips, chips) * 2 + core
        return send(held(h) if s == 0 else chunk(h, j), chunk(h, j), sx.at[h, s], qx.at[h, s], sibling)

    own_o = [pltpu.make_async_copy(held(h), chunk(h, g), local.at[4 + h]) for h in range(2)]

    def spread(h):
        for s in range(1, chips):
            along(h, s).start()
        across(h, 0).start()
        own_o[h].start()

    def relay(h):
        for s in range(1, chips):
            j = lax.rem(z - s + chips, chips) * 2 + core
            send(held(h), chunk(h, j), so.at[h, s], qo.at[h, s], sibling).wait_recv()
            across(h, s).start()

    add_up(0)
    turn(0)
    spread(0)
    add_up(1)
    turn(1)
    spread(1)
    relay(0)
    relay(1)
    for h in range(2):
        for s in range(chips):
            j = lax.rem(z - s + chips, chips) * 2 + 1 - core
            send(held(h), chunk(h, j), sx.at[h, s], qx.at[h, s], sibling).wait_recv()
        own_o[h].wait()

    wait_for(rd.at[pl.ds(0, groups - 1)], sd)
    for h in range(2):
        wait_for(arrived.at[h, :, pl.ds(0, devices - 1)], sb.at[h])
        for s in range(1, owners):
            send_c(h, s).wait_send()
        for s in range(1, chips):
            along(h, s).wait_send()
        for s in range(chips):
            across(h, s).wait_send()


def on_device_kernel(image, variance, block_count, slot_start, psf_index, coef_table):
    groups, owners = lax.axis_size("expgrp"), lax.axis_size("patch")
    devices = groups * owners
    rows, columns = image.shape
    slots = owners * NS
    dma = pltpu.SemaphoreType.DMA
    f32 = jnp.float32
    vmem, hbm = pl.BlockSpec(memory_space=pltpu.VMEM), pl.BlockSpec(memory_space=pltpu.HBM)
    return pl.pallas_call(
        functools.partial(kernel, groups, owners),
        out_shape=jax.ShapeDtypeStruct((NS, 2, BLK // 2, columns), f32),
        in_specs=[hbm] * 8,
        out_specs=pl.BlockSpec(memory_space=pl.ANY),
        scratch_shapes=[
            pltpu.VMEM((rows, columns), f32),
            pltpu.VMEM((rows, columns), f32),
            pltpu.SMEM(block_count.shape, jnp.int32),
            pltpu.SMEM(slot_start.shape, jnp.int32),
            pltpu.SMEM(psf_index.shape, jnp.int32),
            pltpu.SMEM(coef_table.shape[::-1], f32),
            pltpu.VMEM((BASES * rows, rows), f32),
            pltpu.VMEM((BASES * (LANES + 2 * SIDE), 2 * LANES), jnp.bfloat16),
            pltpu.VMEM((rows, columns + 2 * SIDE), f32),
            pltpu.VMEM((columns // LANES, rows, LANES), f32),
            pltpu.VMEM((rows // 8, 2, 8, columns), f32),
            pltpu.VMEM((1, 1, LANES), jnp.int32),
            pltpu.VMEM((2, 2, devices, 8, LANES), f32),
            pltpu.VMEM((groups, 1, LANES), jnp.int32),
            pltpu.VMEM((2, 2, slots, LANES), f32),
            pltpu.VMEM((2, BLK // 2, NS, LANES), f32),
            pltpu.VMEM((2, NS * BLK // 2, LANES), f32),
            dma((2,)), dma, dma((2,)), dma,
            dma((2, owners)), dma((2, owners)),
            dma((2, groups // 2)), dma((2, groups // 2)),
            dma((2, groups // 2)), dma((2, groups // 2)),
            dma((6,)), dma((8,)),
        ],
        compiler_params=pltpu.CompilerParams(
            collective_id=0, has_side_effects=True, vmem_limit_bytes=56 * 1024 * 1024
        ),
    )(
        image, variance, block_count, slot_start, psf_index, coef_table.T,
        jnp.asarray(np_row_table()), jnp.asarray(np_column_table()),
    ).reshape(NS * BLK, columns)


def profile(offsets, deviation):
    offset_range = jnp.arange(-KH, KH + 1).astype(jnp.float32)
    total = jnp.sum(jnp.exp(-offset_range * offset_range / (2.0 * deviation * deviation)))
    spacing = offsets.astype(jnp.float32)
    return jnp.where(
        jnp.abs(offsets) <= KH,
        jnp.exp(-spacing * spacing / (2.0 * deviation * deviation)) / total,
        jnp.float32(0.0),
    )


def column_table(tile_width):
    inner_index = jnp.arange(3 * tile_width, dtype=jnp.int32)[:, None]
    outer_index = jnp.arange(tile_width, dtype=jnp.int32)[None, :]
    columns_list = [
        profile(inner_index - tile_width - outer_index, deviation) for deviation in SIGMAS
    ]
    return jnp.concatenate(columns_list, axis=1)


def row_table(height):
    row_index = jnp.arange(height, dtype=jnp.int32)
    return jnp.stack(
        [profile(row_index[None, :] - row_index[:, None], deviation) for deviation in SIGMAS]
    )


def matched(blocks, mixing):
    number, height, columns = blocks.shape
    tile_width = 128
    tile_count = columns // tile_width
    parted = blocks.reshape(number, height, tile_count, tile_width)
    blank = jnp.zeros((number, height, 1, tile_width), jnp.float32)
    behind = jnp.concatenate([blank, parted[:, :, :-1]], axis=2)
    follow = jnp.concatenate([parted[:, :, 1:], blank], axis=2)
    joined = jnp.concatenate([behind, parted, follow], axis=3)
    across = jnp.einsum("nrti,ik->nrtk", joined, column_table(tile_width), precision=highest)
    across = across.reshape(number, height, tile_count, len(SIGMAS), tile_width)
    vertical = mixing[:, :, None, None] * row_table(height)[None]
    result = jnp.einsum("nbrk,nktbc->nrtc", vertical, across, precision=highest)
    return result.reshape(number, height, columns)


def on_device(image, variance, block_count, slot_start, psf_index, coef_table):
    owners = lax.axis_size("patch")
    own_index = lax.axis_index("patch")
    tile_rows, columns = image.shape
    number = tile_rows // BLK
    lookup = (
        jnp.arange(coef_table.shape[0], dtype=jnp.int32)[None, :] == psf_index[:, None]
    ).astype(jnp.float32)
    mixing = jnp.sum(lookup[:, :, None] * coef_table[None, :, :], axis=1)
    own_count = lax.dynamic_index_in_dim(block_count, own_index, 0, keepdims=False)
    before = jnp.arange(owners)[None, :] < jnp.arange(owners)[:, None]
    firsts = jnp.sum(jnp.where(before, own_count[None, :], 0), axis=1)
    places = jnp.arange(CAP, dtype=jnp.int32)
    source = firsts[:, None] + places[None, :]
    filled = places[None, :] < own_count[:, None]

    def arrange(values):
        total = jnp.zeros((owners, CAP, BLK, columns), jnp.float32)
        for n in range(number):
            here = (source == n) & filled
            total = jnp.where(here[:, :, None, None], values[n][None, None], total)
        return total

    image_blocks = image.reshape(number, BLK, columns)
    scale_blocks = variance.reshape(number, BLK, columns)
    raw_blocks = lax.all_to_all(
        arrange(image_blocks), "patch", split_axis=0, concat_axis=0, tiled=True
    )
    raw_scales = lax.all_to_all(
        arrange(scale_blocks), "patch", split_axis=0, concat_axis=0, tiled=True
    )
    senders = raw_blocks.shape[0]
    slot_count = raw_blocks.shape[1]
    present = raw_scales > 0.0
    weights = jnp.where(present, 1.0 / jnp.where(present, raw_scales, 1.0), 0.0)
    spread = jnp.broadcast_to(mixing[:, None, :], (senders, slot_count, mixing.shape[1]))
    smooth = matched(
        raw_blocks.reshape(senders * slot_count, BLK, columns),
        spread.reshape(senders * slot_count, mixing.shape[1]),
    )
    arrived_flux = weights * smooth.reshape(raw_blocks.shape)
    arrived_count = lax.dynamic_index_in_dim(block_count, own_index, 1, keepdims=False)
    arrived_start = lax.dynamic_index_in_dim(slot_start, own_index, 1, keepdims=False)
    slots = jnp.arange(NS, dtype=jnp.int32)
    target = (places[None, :] < arrived_count[:, None])[None] & (
        arrived_start[:, None] + places[None, :] == slots[:, None, None]
    )
    layout = target.astype(jnp.float32)
    flux_sum = jnp.einsum("spj,pjrw->srw", layout, arrived_flux, precision=highest).reshape(
        NS * BLK, columns
    )
    weight_sum = jnp.einsum("spj,pjrw->srw", layout, weights, precision=highest).reshape(
        NS * BLK, columns
    )
    flux_total, weight_total = lax.psum((flux_sum, weight_sum), "expgrp")
    return flux_total / jnp.maximum(weight_total, 1.0)


def route(groups, owners, image, *rest):
    rows, columns = image.shape
    fits = rows == NB * BLK and columns == LANES * groups and BLK == 4 * owners and groups % 2 == 0
    return on_device_kernel(image, *rest) if fits else on_device(image, *rest)


def solution(mesh):
    in_specs = (
        P(("expgrp", "patch"), None),
        P(("expgrp", "patch"), None),
        P("expgrp", None),
        P("expgrp", None),
        P("expgrp"),
        P(),
    )
    out_specs = P("patch", None)
    return jax.shard_map(
        functools.partial(route, mesh.shape["expgrp"], mesh.shape["patch"]),
        mesh=mesh, in_specs=in_specs, out_specs=out_specs, check_vma=False,
    )
```

profile of v0, /device:TPU:25, one launch (start us, length us, event | category | flops | bytes accessed | tf_op | source)
XLA Modules:
  0.0 34.8 jit_solution(14497490969671049893)
XLA Ops:
  0.0 32.5 %shard_map.82 = f32[16,2,8,1024]{3,2,1,0:T(8,128)} custom-call(f32[64,1024]{1,0:T(8,128)} %refs_0_.1, f32[64,1024]{1,0:T(8,128)} %refs_1_.1, s32[4,4]{1,0:T(4,128)} %refs_2_.1, s32[4,4]{1,0:T(4,128)} %refs_3_.1, s32[4]{0:T(128)} %refs_4_.1, f32[3,64]{1,0:T(4,128)} %bitcast.3, f32[192,64]{1,0:T(8,128)} %constant.4.clone.refs_6_, ...), custom_call_target="tpu_custom_call" | custom-call | tf_op jit(solution)/shard_map/pallas_call | solution.py:278
  32.5 2.3 %copy.10 = f32[256,1024]{1,0:T(8,128)} copy(f32[256,1024]{1,0:T(8,128)} %bitcast.2) | data formatting | bytes 2097152
where the time goes:
time: 35 us; the launch traced here: 34.8 us
  Pallas kernels  32.5 us (93%)
  local copies, waits for them, and re-layouts  2.31 us (7%)
    pallas_call x1, Pallas kernels, on_device_kernel(): pl.pallas_call(functools.partial(kernel, groups, owners), out_shape=jax.S...  32.5 us
    unnamed x1, local copies, waits for them, and re-layouts  2.31 us

commit v1 on v0

--- a/solution.py
+++ b/solution.py
@@ -61,10 +61,10 @@
 
 def kernel(groups, owners, *refs):
     inputs, out, stage = refs[:8], refs[8], refs[9:17]
-    (xpad, vbuf, both, dsrc, arrived, rd, cbuf, tbuf, obuf,
-     sb, sd, qb, qd, sc, qc, so, qo, sx, qx, local, fetch) = refs[17:]
+    (xpad, vbuf, wbuf, fbuf, dsrc, warr, farr, rd, cbuf,
+     sw, qw, sf, qf, sd, qd, so, qo, sx, qx, above, local, fetch) = refs[17:]
     loads = [pltpu.make_async_copy(a, b, fetch.at[n]) for n, (a, b) in enumerate(zip(inputs, stage))]
-    for n in (1, 2, 3, 4, 5, 0, 6, 7):
+    for n in (1, 2, 3, 0, 4, 5, 6, 7):
         loads[n].start()
     img, var, count, start, psf, coef, rows_t, cols_t = stage
     g, p = lax.axis_index("expgrp"), lax.axis_index("patch")
@@ -72,14 +72,20 @@
     me = g * owners + p
     columns = img.shape[1]
     tiles = columns // LANES
+    chips = groups // 2
+    plane = 2 * owners
     z, core = g // 2, g % 2
+    low = plane * (z + 1)
+
+    def place_of(k):
+        return (k // owners, lax.rem(k, owners))
 
     barrier = pltpu.get_barrier_semaphore()
 
-    @pl.loop(1, devices)
+    @pl.loop(1, devices - plane * z)
     def _(s):
-        k = lax.rem(me + s, devices)
-        pl.semaphore_signal(barrier, inc=1, device_id=(k // owners, lax.rem(k, owners)), device_id_type=MESH)
+        k = plane * z + lax.rem(me - plane * z + s, devices - plane * z)
+        pl.semaphore_signal(barrier, inc=1, device_id=place_of(k), device_id_type=MESH)
 
     loads[2].wait()
     loads[3].wait()
@@ -99,10 +105,53 @@
     loads[1].wait()
 
     for t in range(tiles):
-        at = slice(t * LANES, (t + 1) * LANES)
-        vbuf[t] = 1.0 / var[:, at]
+        vbuf[t] = 1.0 / var[:, t * LANES:(t + 1) * LANES]
         for r in range(BLK):
-            both[r // 2, 1, (r % 2) * NB:(r % 2) * NB + NB, at] = vbuf[t, pl.ds(r, NB, stride=BLK), :]
+            h, i = r // 8, (r // 2) % 4
+            wbuf[t * owners + i, h, (r % 2) * NB:(r % 2) * NB + NB, :] = vbuf[t, pl.ds(r, NB, stride=BLK), :]
+
+    def send(src, dst, ssem, rsem, k):
+        return pltpu.make_async_remote_copy(
+            src_ref=src, dst_ref=dst, send_sem=ssem, recv_sem=rsem,
+            device_id=place_of(k), device_id_type=MESH,
+        )
+
+    def wait_for(ref, sem):
+        pltpu.make_async_copy(ref, ref, sem).wait()
+
+    def send_d(k):
+        send(dsrc, rd.at[pl.ds(g, 1)], sd, qd, k).start()
+
+    def send_w(k):
+        send(wbuf.at[k], warr.at[me], sw, qw, k).start()
+
+    def send_f(h, k):
+        send(fbuf.at[h, k], farr.at[h, me], sf.at[h], qf.at[h], k).start()
+
+    def to_low(act):
+        @pl.loop(1, low)
+        def _(s):
+            act(lax.rem(me + s, low))
+
+    def to_high(zz, act):
+        @pl.loop(0, plane)
+        def _(s):
+            act(plane * zz + lax.rem(me + s, plane))
+
+    pl.semaphore_wait(barrier, low - 1)
+
+    @pl.loop(0, plane * z)
+    def _(k):
+        pl.semaphore_signal(above.at[z], inc=1, device_id=place_of(k), device_id_type=MESH)
+
+    @pl.loop(1, 2 * (z + 1))
+    def _(s):
+        send_d(lax.rem(g + s, 2 * (z + 1)) * owners + p)
+
+    own = [pltpu.make_async_copy(wbuf.at[me], warr.at[me], local.at[0])]
+    own += [pltpu.make_async_copy(fbuf.at[h, me], farr.at[h, me], local.at[1 + h]) for h in range(2)]
+    to_low(send_w)
+    own[0].start()
 
     xpad[:, :LANES] = jnp.zeros((NB * BLK, LANES), jnp.float32)
     xpad[:, columns:] = jnp.zeros((NB * BLK, LANES), jnp.float32)
@@ -130,39 +179,31 @@
         one = one + dot(windows(yl), cols_t[b * wide:(b + 1) * wide, :LANES])
     smooth = double[:, :LANES] + double[:, LANES:] + one
     for t in range(tiles):
-        at = slice(t * LANES, (t + 1) * LANES)
-        both[:, 0, :, at] = both[:, 1, :, at] * smooth[t * rows:(t + 1) * rows].reshape(rows // 8, 8, LANES)
-
-    pl.semaphore_wait(barrier, devices - 1)
-
-    def send(src, dst, ssem, rsem, k):
-        return pltpu.make_async_remote_copy(
-            src_ref=src, dst_ref=dst, send_sem=ssem, recv_sem=rsem,
-            device_id=(k // owners, lax.rem(k, owners)), device_id_type=MESH,
-        )
-
-    def wait_for(ref, sem):
-        pltpu.make_async_copy(ref, ref, sem).wait()
-
-    def part(h, k):
-        i, j = lax.rem(k, owners), k // owners
-        return both.at[owners * h + i, :, :, pl.ds(pl.multiple_of(j * LANES, LANES), LANES)]
-
-    def send_d(s):
-        return send(dsrc, rd.at[pl.ds(g, 1)], sd, qd, lax.rem(g + s, groups) * owners + p)
-
-    @pl.loop(1, groups)
-    def _(s):
-        send_d(s).start()
-
-    own_b = [pltpu.make_async_copy(part(h, me), arrived.at[h, :, me], local.at[h]) for h in range(2)]
-    for h in range(2):
-        @pl.loop(1, devices)
-        def _(s):
-            k = lax.rem(me + s, devices)
-            send(part(h, k), arrived.at[h, :, me], sb.at[h], qb.at[h], k).start()
-
-        own_b[h].start()
+        for h in range(2):
+            for i in range(owners):
+                k, at = t * owners + i, t * rows + (h * owners + i) * 8
+                fbuf[h, k] = wbuf[k, h] * smooth[at:at + 8]
+
+    to_low(functools.partial(send_f, 0))
+    own[1].start()
+
+    @pl.loop(z + 1, chips)
+    def _(zz):
+        pl.semaphore_wait(above.at[zz], plane)
+
+        @pl.loop(0, 2)
+        def _(c):
+            send_d((2 * zz + c) * owners + p)
+
+        to_high(zz, send_w)
+        to_high(zz, functools.partial(send_f, 0))
+
+    to_low(functools.partial(send_f, 1))
+    own[2].start()
+
+    @pl.loop(z + 1, chips)
+    def _(zz):
+        to_high(zz, functools.partial(send_f, 1))
 
     wait_for(rd.at[pl.ds(0, groups - 1)], qd)
 
@@ -178,93 +219,86 @@
     row = lax.broadcasted_iota(jnp.int32, (2 * slots, many), 0)
     hot = jnp.where(row == goal, 1.0, 0.0).astype(jnp.bfloat16)
 
-    def piece(h, q):
-        return cbuf.at[h, :, pl.ds(pl.multiple_of(q * NS, NS), NS), :]
-
-    def landing(h, q):
-        return tbuf.at[h, pl.ds(2 * q, 2)]
-
-    def send_c(h, s):
-        q = lax.rem(p + s, owners)
-        return send(piece(h, q), landing(h, p), sc.at[h, s], qc.at[h, p], g * owners + q)
-
-    own_c = [pltpu.make_async_copy(piece(h, p), landing(h, p), local.at[2 + h]) for h in range(2)]
+    wait_for(warr.at[pl.ds(0, devices - 1)], qw)
+    own[0].wait()
+    high, low_part = halves(jnp.concatenate([warr[:, h].reshape(many, LANES) for h in range(2)], axis=1))
+    scale = 1.0 / jnp.maximum(dot(hot, high) + dot(hot, low_part), 1.0)
+
+    def piece(h, there, q):
+        k = (2 * there + core) * owners + q
+        return send(cbuf.at[h, q], out.at[h, g, p], so.at[h], qo.at[h, z], k)
+
+    own_o = [pltpu.make_async_copy(cbuf.at[h, p], out.at[h, g, p], local.at[3 + h]) for h in range(2)]
 
     def add_up(h):
-        wait_for(arrived.at[h, :, pl.ds(0, devices - 1)], qb.at[h])
-        own_b[h].wait()
-        flux, weight = arrived[h, 0].reshape(many, LANES), arrived[h, 1].reshape(many, LANES)
-        high, low = halves(jnp.concatenate([flux, weight], axis=1))
-        total = dot(hot, high) + dot(hot, low)
-        ratio = total[:, :LANES] / jnp.maximum(total[:, LANES:], 1.0)
-        for r2 in range(2):
-            cbuf[h, r2] = ratio[r2 * slots:(r2 + 1) * slots]
-        for s in range(1, owners):
-            send_c(h, s).start()
-        own_c[h].start()
-
-    def turn(h):
-        for s in range(1, owners):
-            e = lax.rem(p + s, owners)
-            send(piece(h, p), landing(h, e), sc.at[h, s], qc.at[h, e], g * owners + e).wait_recv()
-        own_c[h].wait()
-        for r in range(BLK // 2):
-            obuf[h, pl.ds(r, NS, stride=BLK // 2), :] = tbuf[h, r]
-
-    def held(h):
-        return obuf.at[h].reshape(NS, BLK // 2, LANES)
-
-    def chunk(h, j):
-        return out.at[:, h, :, pl.ds(pl.multiple_of(j * LANES, LANES), LANES)]
-
-    chips = groups // 2
+        wait_for(farr.at[h, pl.ds(0, devices - 1)], qf.at[h])
+        own[1 + h].wait()
+        high, low_part = halves(farr[h].reshape(many, LANES))
+        ratio = (dot(hot, high) + dot(hot, low_part)) * scale[:, h * LANES:(h + 1) * LANES]
+        for q in range(owners):
+            for r2 in range(2):
+                cbuf[h, q, r2] = ratio[r2 * slots + q * NS:r2 * slots + (q + 1) * NS]
+
+        @pl.loop(1, chips)
+        def _(s):
+            @pl.loop(0, owners)
+            def _(v):
+                piece(h, lax.rem(z + s, chips), lax.rem(p + v, owners)).start()
+
+        @pl.loop(1, owners)
+        def _(v):
+            piece(h, z, lax.rem(p + v, owners)).start()
+
+        own_o[h].start()
+
     sibling = (z * 2 + 1 - core) * owners + p
 
-    def along(h, s):
-        there = lax.rem(z + s, chips) * 2 + core
-        return send(held(h), chunk(h, g), so.at[h, s], qo.at[h, s], there * owners + p)
-
-    def across(h, s):
-        j = lax.rem(z - s + chips, chips) * 2 + core
-        return send(held(h) if s == 0 else chunk(h, j), chunk(h, j), sx.at[h, s], qx.at[h, s], sibling)
-
-    own_o = [pltpu.make_async_copy(held(h), chunk(h, g), local.at[4 + h]) for h in range(2)]
-
-    def spread(h):
-        for s in range(1, chips):
-            along(h, s).start()
-        across(h, 0).start()
-        own_o[h].start()
+    def across(h, there, side):
+        j = there * 2 + side
+        return send(out.at[h, j], out.at[h, j], sx.at[h, there], qx.at[h, there], sibling)
 
     def relay(h):
-        for s in range(1, chips):
-            j = lax.rem(z - s + chips, chips) * 2 + core
-            send(held(h), chunk(h, j), so.at[h, s], qo.at[h, s], sibling).wait_recv()
-            across(h, s).start()
+        for s in range(chips):
+            there = lax.rem(z + s, chips)
+            if s == 0:
+                wait_for(out.at[h, g, pl.ds(0, owners - 1)], qo.at[h, z])
+                own_o[h].wait()
+            else:
+                wait_for(out.at[h, there * 2 + core], qo.at[h, there])
+            across(h, there, core).start()
 
     add_up(0)
-    turn(0)
-    spread(0)
     add_up(1)
-    turn(1)
-    spread(1)
     relay(0)
     relay(1)
     for h in range(2):
         for s in range(chips):
-            j = lax.rem(z - s + chips, chips) * 2 + 1 - core
-            send(held(h), chunk(h, j), sx.at[h, s], qx.at[h, s], sibling).wait_recv()
-        own_o[h].wait()
+            across(h, lax.rem(z + s, chips), 1 - core).wait_recv()
 
     wait_for(rd.at[pl.ds(0, groups - 1)], sd)
+    wait_for(warr.at[pl.ds(0, devices - 1)], sw)
     for h in range(2):
-        wait_for(arrived.at[h, :, pl.ds(0, devices - 1)], sb.at[h])
-        for s in range(1, owners):
-            send_c(h, s).wait_send()
+        wait_for(farr.at[h, pl.ds(0, devices - 1)], sf.at[h])
         for s in range(1, chips):
-            along(h, s).wait_send()
-        for s in range(chips):
-            across(h, s).wait_send()
+            wait_for(out.at[h, 0], so.at[h])
+        wait_for(out.at[h, 0, pl.ds(0, owners - 1)], so.at[h])
+        for there in range(chips):
+            across(h, there, core).wait_send()
+
+
+def lay_out(parts, out, flat, sem):
+    copies = []
+    for t in range(flat.shape[0]):
+        at = slice(t * LANES, (t + 1) * LANES)
+        for h in range(2):
+            for i in range(BLK // 4):
+                for r2 in range(2):
+                    flat[t, pl.ds(h * 8 + i * 2 + r2, NS, stride=BLK), :] = parts[h, t, i, r2]
+        copy = pltpu.make_async_copy(flat.at[t], out.at[:, at], sem.at[t])
+        copy.start()
+        copies.append(copy)
+    for copy in copies:
+        copy.wait()
 
 
 def on_device_kernel(image, variance, block_count, slot_start, psf_index, coef_table):
@@ -274,10 +308,10 @@
     slots = owners * NS
     dma = pltpu.SemaphoreType.DMA
     f32 = jnp.float32
-    vmem, hbm = pl.BlockSpec(memory_space=pltpu.VMEM), pl.BlockSpec(memory_space=pltpu.HBM)
-    return pl.pallas_call(
+    hbm = pl.BlockSpec(memory_space=pltpu.HBM)
+    parts = pl.pallas_call(
         functools.partial(kernel, groups, owners),
-        out_shape=jax.ShapeDtypeStruct((NS, 2, BLK // 2, columns), f32),
+        out_shape=pltpu.VMEM((2, groups, owners, 2, NS, LANES), f32),
         in_specs=[hbm] * 8,
         out_specs=pl.BlockSpec(memory_space=pl.ANY),
         scratch_shapes=[
@@ -291,18 +325,18 @@
             pltpu.VMEM((BASES * (LANES + 2 * SIDE), 2 * LANES), jnp.bfloat16),
             pltpu.VMEM((rows, columns + 2 * SIDE), f32),
             pltpu.VMEM((columns // LANES, rows, LANES), f32),
-            pltpu.VMEM((rows // 8, 2, 8, columns), f32),
+            pltpu.VMEM((devices, 2, 8, LANES), f32),
+            pltpu.VMEM((2, devices, 8, LANES), f32),
             pltpu.VMEM((1, 1, LANES), jnp.int32),
-            pltpu.VMEM((2, 2, devices, 8, LANES), f32),
+            pltpu.VMEM((devices, 2, 8, LANES), f32),
+            pltpu.VMEM((2, devices, 8, LANES), f32),
             pltpu.VMEM((groups, 1, LANES), jnp.int32),
-            pltpu.VMEM((2, 2, slots, LANES), f32),
-            pltpu.VMEM((2, BLK // 2, NS, LANES), f32),
-            pltpu.VMEM((2, NS * BLK // 2, LANES), f32),
-            dma((2,)), dma, dma((2,)), dma,
-            dma((2, owners)), dma((2, owners)),
+            pltpu.VMEM((2, owners, 2, NS, LANES), f32),
+            dma, dma, dma((2,)), dma((2,)), dma, dma,
+            dma((2,)), dma((2, groups // 2)),
             dma((2, groups // 2)), dma((2, groups // 2)),
-            dma((2, groups // 2)), dma((2, groups // 2)),
-            dma((6,)), dma((8,)),
+            pltpu.SemaphoreType.REGULAR((groups // 2,)),
+            dma((5,)), dma((8,)),
         ],
         compiler_params=pltpu.CompilerParams(
             collective_id=0, has_side_effects=True, vmem_limit_bytes=56 * 1024 * 1024
@@ -310,7 +344,15 @@
     )(
         image, variance, block_count, slot_start, psf_index, coef_table.T,
         jnp.asarray(np_row_table()), jnp.asarray(np_column_table()),
-    ).reshape(NS * BLK, columns)
+    )
+    return pl.pallas_call(
+        lay_out,
+        out_shape=jax.ShapeDtypeStruct((NS * BLK, columns), f32),
+        in_specs=[pl.BlockSpec(memory_space=pltpu.VMEM)],
+        out_specs=hbm,
+        scratch_shapes=[pltpu.VMEM((columns // LANES, NS * BLK, LANES), f32), dma((columns // LANES,))],
+        compiler_params=pltpu.CompilerParams(vmem_limit_bytes=16 * 1024 * 1024),
+    )(parts)
 
 
 def profile(offsets, deviation):

time: 35 us -> 33 us (0.943)
  the two profiles are of different devices: /device:TPU:25 before, /device:TPU:0 now
where the time goes in v1:
time: 33 us; the launch traced here: 32.8 us
  Pallas kernels  32.8 us (99%)
    pallas_call x1, Pallas kernels, on_device_kernel(): pl.pallas_call(functools.partial(kernel, groups, owners), out_shape=pltpu...  31.8 us
    pallas_call x1, Pallas kernels, on_device_kernel(): pl.pallas_call(lay_out, out_shape=jax.ShapeDtypeStruct((NS * BLK, columns...  1.06 us

profile of v1, /device:TPU:0, one launch (start us, length us, event | category | flops | bytes accessed | tf_op | source)
XLA Modules:
  0.0 32.8 jit_solution(4989046773255610878)
XLA Ops:
  0.0 31.8 %shard_map.82.parts = f32[2,8,4,2,16,128]{5,4,3,2,1,0:T(8,128)S(1)} custom-call(f32[64,1024]{1,0:T(8,128)} %refs_0_.1, f32[64,1024]{1,0:T(8,128)} %refs_1_.1, s32[4,4]{1,0:T(4,128)} %refs_2_.1, s32[4,4]{1,0:T(4,128)} %refs_3_.1, s32[4]{0:T(128)} %refs_4_.1, f32[3,64]{1,0:T(4,128)} %bitcast.1, f32[192,64]{1,0:T(8,128)} %constant.4.clone.refs_6_, ...), custom_call_target="tpu_custom_call" | custom-call | tf_op jit(solution)/shard_map/pallas_call | solution.py:312
  31.8 1.1 %shard_map.83 = f32[256,1024]{1,0:T(8,128)} custom-call(f32[2,8,4,2,16,128]{5,4,3,2,1,0:T(8,128)S(1)} %shard_map.82.parts), custom_call_target="tpu_custom_call" | custom-call | tf_op jit(solution)/shard_map/pallas_call | solution.py:348

commit v2 on v1

--- a/solution.py
+++ b/solution.py
@@ -16,6 +16,9 @@
 NB = 4
 LANES = 128
 SIDE = 64
+SENDS = ((((2,), (1,)), ((2,), (0,)), ((1,), (3,)), ((1,), (2,))), (((1,), (2,), (3,)), ((2,), (3,), (0,)), ((3,), (0,), (1,)), ((0,), (1,), (2,))))
+TAKES = ((((1, None), (2, None), (3, None)), ((2, 0), (0, None), (3, 0)), ((3, None), (1, 3), (0, 3)), ((2, None), (1, None), (0, None))), (((1, None), (2, None), (3, None)), ((2, None), (0, None), (3, None)), ((3, None), (1, None), (0, None)), ((2, None), (1, None), (0, None))))
+PASSES = (((), ((2, 0), (3, 0)), ((1, 3), (0, 3)), ()), ((), (), (), ()))
 
 
 SIGMAS = (0.75, 1.5, 3.0)
@@ -62,7 +65,7 @@
 def kernel(groups, owners, *refs):
     inputs, out, stage = refs[:8], refs[8], refs[9:17]
     (xpad, vbuf, wbuf, fbuf, dsrc, warr, farr, rd, cbuf,
-     sw, qw, sf, qf, sd, qd, so, qo, sx, qx, above, local, fetch) = refs[17:]
+     sw, qw, sf, qf, sd, qd, so, qo, sr, sx, qx, above, local, fetch) = refs[17:]
     loads = [pltpu.make_async_copy(a, b, fetch.at[n]) for n, (a, b) in enumerate(zip(inputs, stage))]
     for n in (1, 2, 3, 0, 4, 5, 6, 7):
         loads[n].start()
@@ -75,16 +78,18 @@
     chips = groups // 2
     plane = 2 * owners
     z, core = g // 2, g % 2
-    low = plane * (z + 1)
+    last = devices - plane
+    late = z == chips - 1
+    known = jnp.where(late, devices, last)
 
     def place_of(k):
         return (k // owners, lax.rem(k, owners))
 
     barrier = pltpu.get_barrier_semaphore()
 
-    @pl.loop(1, devices - plane * z)
+    @pl.loop(1, jnp.where(late, plane, devices))
     def _(s):
-        k = plane * z + lax.rem(me - plane * z + s, devices - plane * z)
+        k = jnp.where(late, last + lax.rem(me - last + s, plane), lax.rem(me + s, devices))
         pl.semaphore_signal(barrier, inc=1, device_id=place_of(k), device_id_type=MESH)
 
     loads[2].wait()
@@ -128,29 +133,29 @@
     def send_f(h, k):
         send(fbuf.at[h, k], farr.at[h, me], sf.at[h], qf.at[h], k).start()
 
-    def to_low(act):
-        @pl.loop(1, low)
+    def to_all(act):
+        @pl.loop(1, devices)
         def _(s):
-            act(lax.rem(me + s, low))
-
-    def to_high(zz, act):
-        @pl.loop(0, plane)
-        def _(s):
-            act(plane * zz + lax.rem(me + s, plane))
-
-    pl.semaphore_wait(barrier, low - 1)
-
-    @pl.loop(0, plane * z)
-    def _(k):
-        pl.semaphore_signal(above.at[z], inc=1, device_id=place_of(k), device_id_type=MESH)
-
-    @pl.loop(1, 2 * (z + 1))
+            act(lax.rem(me + s, devices))
+
+    pl.semaphore_wait(barrier, known - 1)
+
+    @pl.when(late)
+    def _():
+        @pl.loop(0, last)
+        def _(k):
+            pl.semaphore_signal(above, inc=1, device_id=place_of(k), device_id_type=MESH)
+
+    @pl.loop(1, known // owners)
     def _(s):
-        send_d(lax.rem(g + s, 2 * (z + 1)) * owners + p)
+        send_d(lax.rem(g + s, known // owners) * owners + p)
 
     own = [pltpu.make_async_copy(wbuf.at[me], warr.at[me], local.at[0])]
     own += [pltpu.make_async_copy(fbuf.at[h, me], farr.at[h, me], local.at[1 + h]) for h in range(2)]
-    to_low(send_w)
+    @pl.loop(1, known)
+    def _(s):
+        send_w(lax.rem(me + s, known))
+
     own[0].start()
 
     xpad[:, :LANES] = jnp.zeros((NB * BLK, LANES), jnp.float32)
@@ -184,26 +189,21 @@
                 k, at = t * owners + i, t * rows + (h * owners + i) * 8
                 fbuf[h, k] = wbuf[k, h] * smooth[at:at + 8]
 
-    to_low(functools.partial(send_f, 0))
-    own[1].start()
-
-    @pl.loop(z + 1, chips)
-    def _(zz):
-        pl.semaphore_wait(above.at[zz], plane)
+    @pl.when(z < chips - 1)
+    def _():
+        pl.semaphore_wait(above, plane)
 
         @pl.loop(0, 2)
         def _(c):
-            send_d((2 * zz + c) * owners + p)
-
-        to_high(zz, send_w)
-        to_high(zz, functools.partial(send_f, 0))
-
-    to_low(functools.partial(send_f, 1))
-    own[2].start()
-
-    @pl.loop(z + 1, chips)
-    def _(zz):
-        to_high(zz, functools.partial(send_f, 1))
+            send_d((groups - 2 + c) * owners + p)
+
+        @pl.loop(0, plane)
+        def _(s):
+            send_w(last + lax.rem(me + s, plane))
+
+    for h in range(2):
+        to_all(functools.partial(send_f, h))
+        own[1 + h].start()
 
     wait_for(rd.at[pl.ds(0, groups - 1)], qd)
 
@@ -230,6 +230,23 @@
 
     own_o = [pltpu.make_async_copy(cbuf.at[h, p], out.at[h, g, p], local.at[3 + h]) for h in range(2)]
 
+    def on_plane(table, act):
+        for zz, entries in enumerate(table):
+            if entries:
+                @pl.when(z == zz)
+                def _(entries=entries):
+                    for entry in entries:
+                        act(*entry)
+
+    def each_piece(h, act):
+        def to_plane(there):
+            for v in range(owners):
+                act(piece(h, there, lax.rem(p + v, owners)))
+
+        on_plane(SENDS[h], to_plane)
+        for v in range(1, owners):
+            act(piece(h, z, lax.rem(p + v, owners)))
+
     def add_up(h):
         wait_for(farr.at[h, pl.ds(0, devices - 1)], qf.at[h])
         own[1 + h].wait()
@@ -238,17 +255,7 @@
         for q in range(owners):
             for r2 in range(2):
                 cbuf[h, q, r2] = ratio[r2 * slots + q * NS:r2 * slots + (q + 1) * NS]
-
-        @pl.loop(1, chips)
-        def _(s):
-            @pl.loop(0, owners)
-            def _(v):
-                piece(h, lax.rem(z + s, chips), lax.rem(p + v, owners)).start()
-
-        @pl.loop(1, owners)
-        def _(v):
-            piece(h, z, lax.rem(p + v, owners)).start()
-
+        each_piece(h, lambda copy: copy.start())
         own_o[h].start()
 
     sibling = (z * 2 + 1 - core) * owners + p
@@ -257,31 +264,36 @@
         j = there * 2 + side
         return send(out.at[h, j], out.at[h, j], sx.at[h, there], qx.at[h, there], sibling)
 
+    def onward(h, there, to):
+        j = there * 2 + core
+        return send(out.at[h, j], out.at[h, j], sr.at[h, there], qo.at[h, there], (to * 2 + core) * owners + p)
+
+    def take(h, there, to):
+        wait_for(out.at[h, there * 2 + core], qo.at[h, there])
+        if to is not None:
+            onward(h, there, to).start()
+        across(h, there, core).start()
+
     def relay(h):
-        for s in range(chips):
-            there = lax.rem(z + s, chips)
-            if s == 0:
-                wait_for(out.at[h, g, pl.ds(0, owners - 1)], qo.at[h, z])
-                own_o[h].wait()
-            else:
-                wait_for(out.at[h, there * 2 + core], qo.at[h, there])
-            across(h, there, core).start()
+        wait_for(out.at[h, g, pl.ds(0, owners - 1)], qo.at[h, z])
+        own_o[h].wait()
+        across(h, z, core).start()
+        on_plane(TAKES[h], functools.partial(take, h))
 
     add_up(0)
     add_up(1)
     relay(0)
     relay(1)
     for h in range(2):
-        for s in range(chips):
-            across(h, lax.rem(z + s, chips), 1 - core).wait_recv()
+        for there in range(chips):
+            across(h, there, 1 - core).wait_recv()
 
     wait_for(rd.at[pl.ds(0, groups - 1)], sd)
     wait_for(warr.at[pl.ds(0, devices - 1)], sw)
     for h in range(2):
         wait_for(farr.at[h, pl.ds(0, devices - 1)], sf.at[h])
-        for s in range(1, chips):
-            wait_for(out.at[h, 0], so.at[h])
-        wait_for(out.at[h, 0, pl.ds(0, owners - 1)], so.at[h])
+        each_piece(h, lambda copy: copy.wait_send())
+        on_plane(PASSES[h], lambda there, to: onward(h, there, to).wait_send())
         for there in range(chips):
             across(h, there, core).wait_send()
 
@@ -333,9 +345,9 @@
             pltpu.VMEM((groups, 1, LANES), jnp.int32),
             pltpu.VMEM((2, owners, 2, NS, LANES), f32),
             dma, dma, dma((2,)), dma((2,)), dma, dma,
-            dma((2,)), dma((2, groups // 2)),
+            dma((2,)), dma((2, groups // 2)), dma((2, groups // 2)),
             dma((2, groups // 2)), dma((2, groups // 2)),
-            pltpu.SemaphoreType.REGULAR((groups // 2,)),
+            pltpu.SemaphoreType.REGULAR,
             dma((5,)), dma((8,)),
         ],
         compiler_params=pltpu.CompilerParams(

time: 33 us -> 31.5 us (0.955)
  Pallas kernels: 32.8 us -> 31.4 us
    pallas_call x1, Pallas kernels: 31.8 us -> 30.3 us  [on_device_kernel(): pl.pallas_call(functools.partial(kernel, groups, owners), out_shape=pltpu...]
where the time goes in v2:
time: 31.5 us; the launch traced here: 31.4 us
  Pallas kernels  31.4 us (100%)
    pallas_call x1, Pallas kernels, on_device_kernel(): pl.pallas_call(functools.partial(kernel, groups, owners), out_shape=pltpu...  30.3 us
    pallas_call x1, Pallas kernels, on_device_kernel(): pl.pallas_call(lay_out, out_shape=jax.ShapeDtypeStruct((NS * BLK, columns...  1.06 us

profile of v2, /device:TPU:0, one launch (start us, length us, event | category | flops | bytes accessed | tf_op | source)
XLA Modules:
  0.0 31.4 jit_solution(3408645674758571885)
XLA Ops:
  0.0 30.3 %shard_map.82.parts = f32[2,8,4,2,16,128]{5,4,3,2,1,0:T(8,128)S(1)} custom-call(f32[64,1024]{1,0:T(8,128)} %refs_0_.1, f32[64,1024]{1,0:T(8,128)} %refs_1_.1, s32[4,4]{1,0:T(4,128)} %refs_2_.1, s32[4,4]{1,0:T(4,128)} %refs_3_.1, s32[4]{0:T(128)} %refs_4_.1, f32[3,64]{1,0:T(4,128)} %bitcast.1, f32[192,64]{1,0:T(8,128)} %constant.4.clone.refs_6_, ...), custom_call_target="tpu_custom_call" | custom-call | tf_op jit(solution)/shard_map/pallas_call | solution.py:324
  30.3 1.1 %shard_map.83 = f32[256,1024]{1,0:T(8,128)} custom-call(f32[2,8,4,2,16,128]{5,4,3,2,1,0:T(8,128)S(1)} %shard_map.82.parts), custom_call_target="tpu_custom_call" | custom-call | tf_op jit(solution)/shard_map/pallas_call | solution.py:360

commit v3 on v2

--- a/solution.py
+++ b/solution.py
@@ -16,6 +16,8 @@
 NB = 4
 LANES = 128
 SIDE = 64
+EARLY = (((2, 0), (1, 0), (0, 1)), ((2, 0), (0, 0), (1, 1)), ((0, 0), (1, 0), (2, 1)), ((0, 0), (1, 0), (2, 0), (3, 1)))
+ORDER = (((2, 0), (3, 0), (1, 0), (0, 1)), ((2, 0), (3, 0), (1, 1), (0, 0)), ((1, 0), (0, 0), (3, 0), (2, 1)), ((1, 0), (0, 0), (2, 0), (3, 1)))
 SENDS = ((((2,), (1,)), ((2,), (0,)), ((1,), (3,)), ((1,), (2,))), (((1,), (2,), (3,)), ((2,), (3,), (0,)), ((3,), (0,), (1,)), ((0,), (1,), (2,))))
 TAKES = ((((1, None), (2, None), (3, None)), ((2, 0), (0, None), (3, 0)), ((3, None), (1, 3), (0, 3)), ((2, None), (1, None), (0, None))), (((1, None), (2, None), (3, None)), ((2, None), (0, None), (3, None)), ((3, None), (1, None), (0, None)), ((2, None), (1, None), (0, None))))
 PASSES = (((), ((2, 0), (3, 0)), ((1, 3), (0, 3)), ()), ((), (), (), ()))
@@ -64,8 +66,8 @@
 
 def kernel(groups, owners, *refs):
     inputs, out, stage = refs[:8], refs[8], refs[9:17]
-    (xpad, vbuf, wbuf, fbuf, dsrc, warr, farr, rd, cbuf,
-     sw, qw, sf, qf, sd, qd, so, qo, sr, sx, qx, above, local, fetch) = refs[17:]
+    (xpad, vbuf, both, dsrc, arrived, rd, cbuf,
+     sb, qb, sd, qd, so, qo, sr, sx, qx, above, local, fetch) = refs[17:]
     loads = [pltpu.make_async_copy(a, b, fetch.at[n]) for n, (a, b) in enumerate(zip(inputs, stage))]
     for n in (1, 2, 3, 0, 4, 5, 6, 7):
         loads[n].start()
@@ -113,7 +115,7 @@
         vbuf[t] = 1.0 / var[:, t * LANES:(t + 1) * LANES]
         for r in range(BLK):
             h, i = r // 8, (r // 2) % 4
-            wbuf[t * owners + i, h, (r % 2) * NB:(r % 2) * NB + NB, :] = vbuf[t, pl.ds(r, NB, stride=BLK), :]
+            both[h, t * owners + i, 1, (r % 2) * NB:(r % 2) * NB + NB, :] = vbuf[t, pl.ds(r, NB, stride=BLK), :]
 
     def send(src, dst, ssem, rsem, k):
         return pltpu.make_async_remote_copy(
@@ -127,36 +129,24 @@
     def send_d(k):
         send(dsrc, rd.at[pl.ds(g, 1)], sd, qd, k).start()
 
-    def send_w(k):
-        send(wbuf.at[k], warr.at[me], sw, qw, k).start()
-
-    def send_f(h, k):
-        send(fbuf.at[h, k], farr.at[h, me], sf.at[h], qf.at[h], k).start()
-
-    def to_all(act):
-        @pl.loop(1, devices)
-        def _(s):
-            act(lax.rem(me + s, devices))
-
-    pl.semaphore_wait(barrier, known - 1)
-
-    @pl.when(late)
-    def _():
-        @pl.loop(0, last)
-        def _(k):
-            pl.semaphore_signal(above, inc=1, device_id=place_of(k), device_id_type=MESH)
-
-    @pl.loop(1, known // owners)
-    def _(s):
-        send_d(lax.rem(g + s, known // owners) * owners + p)
-
-    own = [pltpu.make_async_copy(wbuf.at[me], warr.at[me], local.at[0])]
-    own += [pltpu.make_async_copy(fbuf.at[h, me], farr.at[h, me], local.at[1 + h]) for h in range(2)]
-    @pl.loop(1, known)
-    def _(s):
-        send_w(lax.rem(me + s, known))
-
-    own[0].start()
+    def send_b(h, k):
+        send(both.at[h, k], arrived.at[h, me], sb.at[h], qb.at[h], k).start()
+
+    def on_plane(table, act):
+        for zz, entries in enumerate(table):
+            if entries:
+                @pl.when(z == zz)
+                def _(entries=entries):
+                    for entry in entries:
+                        act(*entry)
+
+    def to_planes(table, act):
+        def to_plane(there, first):
+            @pl.loop(first, plane)
+            def _(s):
+                act(plane * there + lax.rem(me + s, plane))
+
+        on_plane(table, to_plane)
 
     xpad[:, :LANES] = jnp.zeros((NB * BLK, LANES), jnp.float32)
     xpad[:, columns:] = jnp.zeros((NB * BLK, LANES), jnp.float32)
@@ -166,28 +156,47 @@
     for n in (4, 5, 6):
         loads[n].wait()
     which = psf[p]
-    rows = NB * BLK
-    ah, al = halves(
-        jnp.concatenate([rows_t[b * rows:(b + 1) * rows, :] * coef[b, which] for b in range(BASES)], axis=0)
-    )
-    yh, yl = halves(dot(ah, xh) + dot(al, xh) + dot(ah, xl))
+    loads[7].wait()
+    rows, part = NB * BLK, NB * BLK // 2
     wide = LANES + 2 * SIDE
-    loads[7].wait()
-    double = jnp.zeros((tiles * rows, 2 * LANES), jnp.float32)
-    one = jnp.zeros((tiles * rows, LANES), jnp.float32)
-    for b in range(BASES):
-        def windows(y):
-            return jnp.concatenate(
-                [y[b * rows:(b + 1) * rows, t * LANES:t * LANES + wide] for t in range(tiles)], axis=0
-            )
-        double = double + dot(windows(yh), cols_t[b * wide:(b + 1) * wide, :])
-        one = one + dot(windows(yl), cols_t[b * wide:(b + 1) * wide, :LANES])
-    smooth = double[:, :LANES] + double[:, LANES:] + one
-    for t in range(tiles):
-        for h in range(2):
+
+    def smooth(h):
+        ah, al = halves(jnp.concatenate(
+            [rows_t[b * rows + h * part:b * rows + (h + 1) * part, :] * coef[b, which] for b in range(BASES)], axis=0
+        ))
+        yh, yl = halves(dot(ah, xh) + dot(al, xh) + dot(ah, xl))
+        double = jnp.zeros((tiles * part, 2 * LANES), jnp.float32)
+        one = jnp.zeros((tiles * part, LANES), jnp.float32)
+        for b in range(BASES):
+            def windows(y):
+                return jnp.concatenate(
+                    [y[b * part:(b + 1) * part, t * LANES:t * LANES + wide] for t in range(tiles)], axis=0
+                )
+            double = double + dot(windows(yh), cols_t[b * wide:(b + 1) * wide, :])
+            one = one + dot(windows(yl), cols_t[b * wide:(b + 1) * wide, :LANES])
+        total = double[:, :LANES] + double[:, LANES:] + one
+        for t in range(tiles):
             for i in range(owners):
-                k, at = t * owners + i, t * rows + (h * owners + i) * 8
-                fbuf[h, k] = wbuf[k, h] * smooth[at:at + 8]
+                k, at = t * owners + i, t * part + i * 8
+                both[h, k, 0] = both[h, k, 1] * total[at:at + 8]
+
+    smooth(0)
+    pl.semaphore_wait(barrier, known - 1)
+
+    @pl.when(late)
+    def _():
+        @pl.loop(0, last)
+        def _(k):
+            pl.semaphore_signal(above, inc=1, device_id=place_of(k), device_id_type=MESH)
+
+    @pl.loop(1, known // owners)
+    def _(s):
+        send_d(lax.rem(g + s, known // owners) * owners + p)
+
+    own = [pltpu.make_async_copy(both.at[h, me], arrived.at[h, me], local.at[h]) for h in range(2)]
+    to_planes(EARLY, functools.partial(send_b, 0))
+    own[0].start()
+    smooth(1)
 
     @pl.when(z < chips - 1)
     def _():
@@ -199,11 +208,10 @@
 
         @pl.loop(0, plane)
         def _(s):
-            send_w(last + lax.rem(me + s, plane))
-
-    for h in range(2):
-        to_all(functools.partial(send_f, h))
-        own[1 + h].start()
+            send_b(0, last + lax.rem(me + s, plane))
+
+    to_planes(ORDER, functools.partial(send_b, 1))
+    own[1].start()
 
     wait_for(rd.at[pl.ds(0, groups - 1)], qd)
 
@@ -219,24 +227,11 @@
     row = lax.broadcasted_iota(jnp.int32, (2 * slots, many), 0)
     hot = jnp.where(row == goal, 1.0, 0.0).astype(jnp.bfloat16)
 
-    wait_for(warr.at[pl.ds(0, devices - 1)], qw)
-    own[0].wait()
-    high, low_part = halves(jnp.concatenate([warr[:, h].reshape(many, LANES) for h in range(2)], axis=1))
-    scale = 1.0 / jnp.maximum(dot(hot, high) + dot(hot, low_part), 1.0)
-
     def piece(h, there, q):
         k = (2 * there + core) * owners + q
         return send(cbuf.at[h, q], out.at[h, g, p], so.at[h], qo.at[h, z], k)
 
-    own_o = [pltpu.make_async_copy(cbuf.at[h, p], out.at[h, g, p], local.at[3 + h]) for h in range(2)]
-
-    def on_plane(table, act):
-        for zz, entries in enumerate(table):
-            if entries:
-                @pl.when(z == zz)
-                def _(entries=entries):
-                    for entry in entries:
-                        act(*entry)
+    own_o = [pltpu.make_async_copy(cbuf.at[h, p], out.at[h, g, p], local.at[2 + h]) for h in range(2)]
 
     def each_piece(h, act):
         def to_plane(there):
@@ -248,10 +243,11 @@
             act(piece(h, z, lax.rem(p + v, owners)))
 
     def add_up(h):
-        wait_for(farr.at[h, pl.ds(0, devices - 1)], qf.at[h])
-        own[1 + h].wait()
-        high, low_part = halves(farr[h].reshape(many, LANES))
-        ratio = (dot(hot, high) + dot(hot, low_part)) * scale[:, h * LANES:(h + 1) * LANES]
+        wait_for(arrived.at[h, pl.ds(0, devices - 1)], qb.at[h])
+        own[h].wait()
+        high, low_part = halves(jnp.concatenate([arrived[h, :, n].reshape(many, LANES) for n in range(2)], axis=1))
+        total = dot(hot, high) + dot(hot, low_part)
+        ratio = total[:, :LANES] / jnp.maximum(total[:, LANES:], 1.0)
         for q in range(owners):
             for r2 in range(2):
                 cbuf[h, q, r2] = ratio[r2 * slots + q * NS:r2 * slots + (q + 1) * NS]
@@ -289,9 +285,8 @@
             across(h, there, 1 - core).wait_recv()
 
     wait_for(rd.at[pl.ds(0, groups - 1)], sd)
-    wait_for(warr.at[pl.ds(0, devices - 1)], sw)
     for h in range(2):
-        wait_for(farr.at[h, pl.ds(0, devices - 1)], sf.at[h])
+        wait_for(arrived.at[h, pl.ds(0, devices - 1)], sb.at[h])
         each_piece(h, lambda copy: copy.wait_send())
         on_plane(PASSES[h], lambda there, to: onward(h, there, to).wait_send())
         for there in range(chips):
@@ -337,18 +332,16 @@
             pltpu.VMEM((BASES * (LANES + 2 * SIDE), 2 * LANES), jnp.bfloat16),
             pltpu.VMEM((rows, columns + 2 * SIDE), f32),
             pltpu.VMEM((columns // LANES, rows, LANES), f32),
-            pltpu.VMEM((devices, 2, 8, LANES), f32),
-            pltpu.VMEM((2, devices, 8, LANES), f32),
+            pltpu.VMEM((2, devices, 2, 8, LANES), f32),
             pltpu.VMEM((1, 1, LANES), jnp.int32),
-            pltpu.VMEM((devices, 2, 8, LANES), f32),
-            pltpu.VMEM((2, devices, 8, LANES), f32),
+            pltpu.VMEM((2, devices, 2, 8, LANES), f32),
             pltpu.VMEM((groups, 1, LANES), jnp.int32),
             pltpu.VMEM((2, owners, 2, NS, LANES), f32),
-            dma, dma, dma((2,)), dma((2,)), dma, dma,
+            dma((2,)), dma((2,)), dma, dma,
             dma((2,)), dma((2, groups // 2)), dma((2, groups // 2)),
             dma((2, groups // 2)), dma((2, groups // 2)),
             pltpu.SemaphoreType.REGULAR,
-            dma((5,)), dma((8,)),
+            dma((4,)), dma((8,)),
         ],
         compiler_params=pltpu.CompilerParams(
             collective_id=0, has_side_effects=True, vmem_limit_bytes=56 * 1024 * 1024

time: 31.5 us -> 30.8 us (0.978)
  Pallas kernels: 31.4 us -> 30.6 us
    pallas_call x1, Pallas kernels: 30.3 us -> 29.6 us  [on_device_kernel(): pl.pallas_call(functools.partial(kernel, groups, owners), out_shape=pltpu...]
where the time goes in v3:
time: 30.8 us; the launch traced here: 30.6 us
  Pallas kernels  30.6 us (99%)
    pallas_call x1, Pallas kernels, on_device_kernel(): pl.pallas_call(functools.partial(kernel, groups, owners), out_shape=pltpu...  29.6 us
    pallas_call x1, Pallas kernels, on_device_kernel(): pl.pallas_call(lay_out, out_shape=jax.ShapeDtypeStruct((NS * BLK, columns...  1.06 us

profile of v3, /device:TPU:0, one launch (start us, length us, event | category | flops | bytes accessed | tf_op | source)
XLA Modules:
  0.0 30.6 jit_solution(15840853626748739054)
XLA Ops:
  0.0 29.6 %shard_map.82.parts = f32[2,8,4,2,16,128]{5,4,3,2,1,0:T(8,128)S(1)} custom-call(f32[64,1024]{1,0:T(8,128)} %refs_0_.1, f32[64,1024]{1,0:T(8,128)} %refs_1_.1, s32[4,4]{1,0:T(4,128)} %refs_2_.1, s32[4,4]{1,0:T(4,128)} %refs_3_.1, s32[4]{0:T(128)} %refs_4_.1, f32[3,64]{1,0:T(4,128)} %bitcast.1, f32[192,64]{1,0:T(8,128)} %constant.4.clone.refs_6_, ...), custom_call_target="tpu_custom_call" | custom-call | tf_op jit(solution)/shard_map/pallas_call | solution.py:319
  29.6 1.1 %shard_map.83 = f32[256,1024]{1,0:T(8,128)} custom-call(f32[2,8,4,2,16,128]{5,4,3,2,1,0:T(8,128)S(1)} %shard_map.82.parts), custom_call_target="tpu_custom_call" | custom-call | tf_op jit(solution)/shard_map/pallas_call | solution.py:353

commit v4 on v3

--- a/solution.py
+++ b/solution.py
@@ -17,10 +17,10 @@
 LANES = 128
 SIDE = 64
 EARLY = (((2, 0), (1, 0), (0, 1)), ((2, 0), (0, 0), (1, 1)), ((0, 0), (1, 0), (2, 1)), ((0, 0), (1, 0), (2, 0), (3, 1)))
-ORDER = (((2, 0), (3, 0), (1, 0), (0, 1)), ((2, 0), (3, 0), (1, 1), (0, 0)), ((1, 0), (0, 0), (3, 0), (2, 1)), ((1, 0), (0, 0), (2, 0), (3, 1)))
-SENDS = ((((2,), (1,)), ((2,), (0,)), ((1,), (3,)), ((1,), (2,))), (((1,), (2,), (3,)), ((2,), (3,), (0,)), ((3,), (0,), (1,)), ((0,), (1,), (2,))))
-TAKES = ((((1, None), (2, None), (3, None)), ((2, 0), (0, None), (3, 0)), ((3, None), (1, 3), (0, 3)), ((2, None), (1, None), (0, None))), (((1, None), (2, None), (3, None)), ((2, None), (0, None), (3, None)), ((3, None), (1, None), (0, None)), ((2, None), (1, None), (0, None))))
-PASSES = (((), ((2, 0), (3, 0)), ((1, 3), (0, 3)), ()), ((), (), (), ()))
+ORDER = (((2, 0), (3, 0), (0, 1), (1, 0)), ((2, 0), (3, 0), (1, 1), (0, 0)), ((1, 0), (0, 0), (2, 1), (3, 0)), ((1, 0), (0, 0), (3, 1), (2, 0)))
+SENDS = ((((2,), (1,)), ((2,), (3,), (0,)), ((1,), (0,), (3,)), ((1,), (2,))), (((1,), (2,), (3,)), ((2,), (3,), (0,)), ((3,), (0,), (1,)), ((0,), (1,), (2,))))
+TAKES = ((((1, None), (2, None), (3, None)), ((2, None), (0, None), (3, 0)), ((3, None), (1, None), (0, 3)), ((2, None), (1, None), (0, None))), (((1, None), (2, None), (3, None)), ((2, None), (0, None), (3, None)), ((3, None), (1, None), (0, None)), ((2, None), (1, None), (0, None))))
+PASSES = (((), ((3, 0),), ((0, 3),), ()), ((), (), (), ()))
 
 
 SIGMAS = (0.75, 1.5, 3.0)

time: 30.8 us -> 30.3 us (0.984)
  Pallas kernels: 30.6 us -> 30.1 us
    pallas_call x1, Pallas kernels: 29.6 us -> 29 us  [on_device_kernel(): pl.pallas_call(functools.partial(kernel, groups, owners), out_shape=pltpu...]
where the time goes in v4:
time: 30.3 us; the launch traced here: 30.1 us
  Pallas kernels  30.1 us (99%)
    pallas_call x1, Pallas kernels, on_device_kernel(): pl.pallas_call(functools.partial(kernel, groups, owners), out_shape=pltpu...  29 us
    pallas_call x1, Pallas kernels, on_device_kernel(): pl.pallas_call(lay_out, out_shape=jax.ShapeDtypeStruct((NS * BLK, columns...  1.06 us

profile of v4, /device:TPU:0, one launch (start us, length us, event | category | flops | bytes accessed | tf_op | source)
XLA Modules:
  0.0 30.1 jit_solution(10334023788122041279)
XLA Ops:
  0.0 29.0 %shard_map.82.parts = f32[2,8,4,2,16,128]{5,4,3,2,1,0:T(8,128)S(1)} custom-call(f32[64,1024]{1,0:T(8,128)} %refs_0_.1, f32[64,1024]{1,0:T(8,128)} %refs_1_.1, s32[4,4]{1,0:T(4,128)} %refs_2_.1, s32[4,4]{1,0:T(4,128)} %refs_3_.1, s32[4]{0:T(128)} %refs_4_.1, f32[3,64]{1,0:T(4,128)} %bitcast.1, f32[192,64]{1,0:T(8,128)} %constant.4.clone.refs_6_, ...), custom_call_target="tpu_custom_call" | custom-call | tf_op jit(solution)/shard_map/pallas_call | solution.py:319
  29.0 1.1 %shard_map.83 = f32[256,1024]{1,0:T(8,128)} custom-call(f32[2,8,4,2,16,128]{5,4,3,2,1,0:T(8,128)S(1)} %shard_map.82.parts), custom_call_target="tpu_custom_call" | custom-call | tf_op jit(solution)/shard_map/pallas_call | solution.py:353

commit v5 on v4

--- a/solution.py
+++ b/solution.py
@@ -20,6 +20,7 @@
 ORDER = (((2, 0), (3, 0), (0, 1), (1, 0)), ((2, 0), (3, 0), (1, 1), (0, 0)), ((1, 0), (0, 0), (2, 1), (3, 0)), ((1, 0), (0, 0), (3, 1), (2, 0)))
 SENDS = ((((2,), (1,)), ((2,), (3,), (0,)), ((1,), (0,), (3,)), ((1,), (2,))), (((1,), (2,), (3,)), ((2,), (3,), (0,)), ((3,), (0,), (1,)), ((0,), (1,), (2,))))
 TAKES = ((((1, None), (2, None), (3, None)), ((2, None), (0, None), (3, 0)), ((3, None), (1, None), (0, 3)), ((2, None), (1, None), (0, None))), (((1, None), (2, None), (3, None)), ((2, None), (0, None), (3, None)), ((3, None), (1, None), (0, None)), ((2, None), (1, None), (0, None))))
+COUNTS = ((((2,),), ((3,),), ((3,),), ((2,),)), (((3,),), ((3,),), ((3,),), ((3,),)))
 PASSES = (((), ((3, 0),), ((0, 3),), ()), ((), (), (), ()))
 
 
@@ -144,7 +145,7 @@
         def to_plane(there, first):
             @pl.loop(first, plane)
             def _(s):
-                act(plane * there + lax.rem(me + s, plane))
+                act(plane * there + (lax.rem(me, plane) ^ s))
 
         on_plane(table, to_plane)
 
@@ -258,7 +259,7 @@
 
     def across(h, there, side):
         j = there * 2 + side
-        return send(out.at[h, j], out.at[h, j], sx.at[h, there], qx.at[h, there], sibling)
+        return send(out.at[h, j], out.at[h, j], sx.at[h], qx.at[h], sibling)
 
     def onward(h, there, to):
         j = there * 2 + core
@@ -276,21 +277,23 @@
         across(h, z, core).start()
         on_plane(TAKES[h], functools.partial(take, h))
 
+    def drain(h):
+        on_plane(COUNTS[h], lambda n: wait_for(out.at[h, pl.ds(0, n)], so.at[h]))
+        wait_for(out.at[h, 0, pl.ds(0, owners - 1)], so.at[h])
+        on_plane(PASSES[h], lambda there, to: onward(h, there, to).wait_send())
+
     add_up(0)
     add_up(1)
-    relay(0)
-    relay(1)
-    for h in range(2):
-        for there in range(chips):
-            across(h, there, 1 - core).wait_recv()
-
     wait_for(rd.at[pl.ds(0, groups - 1)], sd)
     for h in range(2):
         wait_for(arrived.at[h, pl.ds(0, devices - 1)], sb.at[h])
-        each_piece(h, lambda copy: copy.wait_send())
-        on_plane(PASSES[h], lambda there, to: onward(h, there, to).wait_send())
-        for there in range(chips):
-            across(h, there, core).wait_send()
+    relay(0)
+    drain(0)
+    relay(1)
+    drain(1)
+    for sem in (qx, sx):
+        for h in range(2):
+            wait_for(out.at[h, pl.ds(0, chips)], sem.at[h])
 
 
 def lay_out(parts, out, flat, sem):
@@ -339,7 +342,7 @@
             pltpu.VMEM((2, owners, 2, NS, LANES), f32),
             dma((2,)), dma((2,)), dma, dma,
             dma((2,)), dma((2, groups // 2)), dma((2, groups // 2)),
-            dma((2, groups // 2)), dma((2, groups // 2)),
+            dma((2,)), dma((2,)),
             pltpu.SemaphoreType.REGULAR,
             dma((4,)), dma((8,)),
         ],

time: 30.3 us -> 30.1 us (level)
  no operation moved by 1% of the time
where the time goes in v5:
time: 30.1 us; the launch traced here: 29.8 us
  Pallas kernels  29.8 us (99%)
    pallas_call x1, Pallas kernels, on_device_kernel(): pl.pallas_call(functools.partial(kernel, groups, owners), out_shape=pltpu...  28.7 us
    pallas_call x1, Pallas kernels, on_device_kernel(): pl.pallas_call(lay_out, out_shape=jax.ShapeDtypeStruct((NS * BLK, columns...  1.06 us

profile of v5, /device:TPU:0, one launch (start us, length us, event | category | flops | bytes accessed | tf_op | source)
XLA Modules:
  0.0 29.8 jit_solution(7510819691868121390)
XLA Ops:
  0.0 28.7 %shard_map.82.parts = f32[2,8,4,2,16,128]{5,4,3,2,1,0:T(8,128)S(1)} custom-call(f32[64,1024]{1,0:T(8,128)} %refs_0_.1, f32[64,1024]{1,0:T(8,128)} %refs_1_.1, s32[4,4]{1,0:T(4,128)} %refs_2_.1, s32[4,4]{1,0:T(4,128)} %refs_3_.1, s32[4]{0:T(128)} %refs_4_.1, f32[3,64]{1,0:T(4,128)} %bitcast.1, f32[192,64]{1,0:T(8,128)} %constant.4.clone.refs_6_, ...), custom_call_target="tpu_custom_call" | custom-call | tf_op jit(solution)/shard_map/pallas_call | solution.py:322
  28.7 1.1 %shard_map.83 = f32[256,1024]{1,0:T(8,128)} custom-call(f32[2,8,4,2,16,128]{5,4,3,2,1,0:T(8,128)S(1)} %shard_map.82.parts), custom_call_target="tpu_custom_call" | custom-call | tf_op jit(solution)/shard_map/pallas_call | solution.py:356

commit v6 on v5

--- a/solution.py
+++ b/solution.py
@@ -197,8 +197,6 @@
     own = [pltpu.make_async_copy(both.at[h, me], arrived.at[h, me], local.at[h]) for h in range(2)]
     to_planes(EARLY, functools.partial(send_b, 0))
     own[0].start()
-    smooth(1)
-
     @pl.when(z < chips - 1)
     def _():
         pl.semaphore_wait(above, plane)
@@ -211,6 +209,7 @@
         def _(s):
             send_b(0, last + lax.rem(me + s, plane))
 
+    smooth(1)
     to_planes(ORDER, functools.partial(send_b, 1))
     own[1].start()
 
@@ -239,9 +238,9 @@
             for v in range(owners):
                 act(piece(h, there, lax.rem(p + v, owners)))
 
-        on_plane(SENDS[h], to_plane)
         for v in range(1, owners):
             act(piece(h, z, lax.rem(p + v, owners)))
+        on_plane(SENDS[h], to_plane)
 
     def add_up(h):
         wait_for(arrived.at[h, pl.ds(0, devices - 1)], qb.at[h])

time: 30.1 us -> 30.1 us (level)
  no operation moved by 1% of the time
where the time goes in v6:
time: 30.1 us; the launch traced here: 29.8 us
  Pallas kernels  29.8 us (99%)
    pallas_call x1, Pallas kernels, on_device_kernel(): pl.pallas_call(functools.partial(kernel, groups, owners), out_shape=pltpu...  28.7 us
    pallas_call x1, Pallas kernels, on_device_kernel(): pl.pallas_call(lay_out, out_shape=jax.ShapeDtypeStruct((NS * BLK, columns...  1.06 us

profile of v6, /device:TPU:0, one launch (start us, length us, event | category | flops | bytes accessed | tf_op | source)
XLA Modules:
  0.0 29.8 jit_solution(17570138471321919013)
XLA Ops:
  0.0 28.7 %shard_map.82.parts = f32[2,8,4,2,16,128]{5,4,3,2,1,0:T(8,128)S(1)} custom-call(f32[64,1024]{1,0:T(8,128)} %refs_0_.1, f32[64,1024]{1,0:T(8,128)} %refs_1_.1, s32[4,4]{1,0:T(4,128)} %refs_2_.1, s32[4,4]{1,0:T(4,128)} %refs_3_.1, s32[4]{0:T(128)} %refs_4_.1, f32[3,64]{1,0:T(4,128)} %bitcast.1, f32[192,64]{1,0:T(8,128)} %constant.4.clone.refs_6_, ...), custom_call_target="tpu_custom_call" | custom-call | tf_op jit(solution)/shard_map/pallas_call | solution.py:321
  28.7 1.1 %shard_map.83 = f32[256,1024]{1,0:T(8,128)} custom-call(f32[2,8,4,2,16,128]{5,4,3,2,1,0:T(8,128)S(1)} %shard_map.82.parts), custom_call_target="tpu_custom_call" | custom-call | tf_op jit(solution)/shard_map/pallas_call | solution.py:355
